TPU v7x, 32 devices: a whole 2x2x4 slice. The times are simulated.
32 devices in a mesh: batch: 4 (over x, core), frame: 8 (over z, y).
Axes of the slice: x: 2, y: 2, z: 4, core: 2. Of those that a mesh axis runs over, the one named last changes fastest.
Arguments:
- latents: bfloat16 [4, 4096, 384], P('batch', 'frame'), may hold values from -6 to 6
- time_embed: bfloat16 [4, 4, 384], P('batch'), may hold values from -6 to 6
- text_states: bfloat16 [4, 4, 128, 512], P('batch'), may hold values from -6 to 6
- text_len: int32 [4, 4], P('batch'), may hold values from 4 to 128
- clip_len: int32 [4, 4], P('batch'), may hold values from 1 to 4093, as said below
- cotangent: bfloat16 [4, 4096, 384], P('batch', 'frame'), may hold values from -6 to 6
- w_ada: bfloat16 [384, 2304], replicated, may hold values from -0.3125 to 0.3125
- b_ada: float32 [2304], replicated, may hold values from -3 to 3
- w_qkv: bfloat16 [384, 1152], replicated, may hold values from -0.3125 to 0.3125
- w_ao: bfloat16 [384, 384], replicated, may hold values from -1.25 to 1.25
- gain_cross: float32 [384], replicated, may hold values from 0.1 to 1.9
- w_cq: bfloat16 [384, 384], replicated, may hold values from -0.3125 to 0.3125
- w_ckv: bfloat16 [512, 768], replicated, may hold values from -0.25 to 0.25
- w_co: bfloat16 [384, 384], replicated, may hold values from -0.875 to 0.875
- w_up: bfloat16 [384, 1536], replicated, may hold values from -0.3125 to 0.3125
- w_down: bfloat16 [1536, 384], replicated, may hold values from -0.15625 to 0.15625
Outputs:
- mixed: bfloat16 [4, 4096, 384], P('batch', 'frame')
- grad_latents: bfloat16 [4, 4096, 384], P('batch', 'frame')
- grad_w_ada: float32 [384, 2304], replicated
- grad_b_ada: float32 [2304], replicated
- grad_w_qkv: float32 [384, 1152], replicated
- grad_w_ao: float32 [384, 384], replicated
- grad_gain_cross: float32 [384], replicated
- grad_w_cq: float32 [384, 384], replicated
- grad_w_ckv: float32 [512, 768], replicated
- grad_w_co: float32 [384, 384], replicated
- grad_w_up: float32 [384, 1536], replicated
- grad_w_down: float32 [1536, 384], replicated
Inputs may be any that keep to these rules, and one draw needn't show every extreme that they name: `clip_len`: in each group the 4 lengths sum to at most 4096; one clip, at a place drawn from the seed, begins within the first 512 frames and ends within the last 512; the frames after the clips are padding. In one group, drawn from the seed, there is no padding and the other clips have one frame each.
All inputs are finite; a program needn't handle non-finite values.
Results may differ from a plain program's by a relative error of at most 0.025.
Values may be sent and summed in bfloat16 or wider, within the bound.
A program may use at most 320 MiB of HBM per device.

v0:
```python
import math

import jax
import jax.numpy as jnp
from jax import lax
from jax.sharding import PartitionSpec as P

HEADS = 6


highest = lax.Precision.HIGHEST
eps_norm = 1e-06
neg_fill = -1e30


def layer_norm(values):
    center = values - jnp.mean(values, axis=-1, keepdims=True)
    inverse = lax.rsqrt(jnp.mean(center * center, axis=-1, keepdims=True) + eps_norm)
    return (center * inverse, inverse)


def norm_back(grad, normed, inverse):
    mean_grad = jnp.mean(grad, axis=-1, keepdims=True)
    mean_prod = jnp.mean(grad * normed, axis=-1, keepdims=True)
    return (grad - mean_grad - normed * mean_prod) * inverse


def ids_at(positions, clip_ends):
    return jnp.sum((positions[:, None] >= clip_ends[None, :]).astype(jnp.int32), axis=1)


def split_heads(matrix, head_count):
    return matrix.reshape(matrix.shape[0], head_count, matrix.shape[1] // head_count).transpose(
        1, 0, 2
    )


def join_heads(stacked):
    return stacked.transpose(1, 0, 2).reshape(stacked.shape[1], stacked.shape[0] * stacked.shape[2])


def block_rows(row_count):
    return math.gcd(row_count, 1024)


def masked_scores(queries_h, keys_h, key_ids, query_ids, clip_count):
    head_size = queries_h.shape[2]
    scores = jnp.einsum(
        "hqd,hkd->hqk", queries_h, keys_h, preferred_element_type=jnp.float32
    ) * head_size ** (-0.5)
    allowed = (query_ids[:, None] == key_ids[None, :]) & (key_ids[None, :] < clip_count)
    return jnp.where(allowed[None], scores, neg_fill)


def split_blocks(kv_rows, key_ids):
    row_count = kv_rows.shape[0]
    block_size = block_rows(row_count)
    kv_blocks = kv_rows.reshape(row_count // block_size, block_size, kv_rows.shape[1])
    id_blocks = key_ids.reshape(row_count // block_size, block_size)
    return (kv_blocks, id_blocks)


def fold_keys(carried, kv_rows, key_ids, queries_h, query_ids, clip_count):
    head_count = queries_h.shape[0]
    model_width = kv_rows.shape[1] // 2
    kv_blocks, id_blocks = split_blocks(kv_rows, key_ids)

    def per_block(state_now, element):
        running_max, row_sum, weighted = state_now
        kv_block, id_block = element
        keys_h = split_heads(kv_block[:, :model_width], head_count)
        values_h = split_heads(kv_block[:, model_width:], head_count)
        scores = masked_scores(queries_h, keys_h, id_block, query_ids, clip_count)
        new_max = jnp.maximum(running_max, jnp.max(scores, axis=-1))
        factor = jnp.exp(running_max - new_max)
        weights_now = jnp.exp(scores - new_max[..., None])
        row_sum = row_sum * factor + jnp.sum(weights_now, axis=-1)
        weighted = weighted * factor[..., None] + jnp.einsum(
            "hqk,hkd->hqd",
            weights_now.astype(jnp.bfloat16),
            values_h,
            preferred_element_type=jnp.float32,
        )
        return ((new_max, row_sum, weighted), None)

    return lax.scan(per_block, carried, (kv_blocks, id_blocks))[0]


def per_device(
    latents,
    time_embed,
    text_states,
    text_len,
    clip_len,
    cotangent,
    w_ada,
    b_ada,
    w_qkv,
    w_ao,
    gain_cross,
    w_cq,
    w_ckv,
    w_co,
    w_up,
    w_down,
):
    frames = latents.shape[1]
    model_width = latents.shape[2]
    clip_count = time_embed.shape[1]
    text_slots = text_states.shape[2]
    head_count = HEADS
    head_size = model_width // head_count
    score_scale = head_size ** (-0.5)
    group_frames = frames * lax.axis_size("frame")
    clip_ends = jnp.cumsum(clip_len[0])
    first_frame = lax.axis_index("frame") * frames
    local_ids = ids_at(first_frame + jnp.arange(frames, dtype=jnp.int32), clip_ends)
    frame_valid = (local_ids < clip_count).astype(jnp.float32)[:, None]
    onehot = (local_ids[:, None] == jnp.arange(clip_count, dtype=jnp.int32)[None, :]).astype(
        jnp.float32
    )
    inputs = latents[0].astype(jnp.float32)
    time_low = jax.nn.silu(time_embed[0].astype(jnp.float32)).astype(jnp.bfloat16)
    modulation = jnp.dot(time_low, w_ada, preferred_element_type=jnp.float32) + b_ada
    frame_mod = jnp.dot(onehot, modulation, precision=highest)
    shift_attn, scale_attn, gate_attn, shift_mlp, scale_mlp, gate_mlp = jnp.split(
        frame_mod, 6, axis=1
    )
    normed_attn, inverse_attn = layer_norm(inputs)
    modulated = (normed_attn * (1.0 + scale_attn) + shift_attn).astype(jnp.bfloat16)
    projected = jnp.dot(modulated, w_qkv, preferred_element_type=jnp.float32).astype(jnp.bfloat16)
    queries_h = split_heads(projected[:, :model_width], head_count)
    kv_local = projected[:, model_width:]
    initial = (
        jnp.full((head_count, frames), neg_fill, jnp.float32),
        jnp.zeros((head_count, frames), jnp.float32),
        jnp.zeros((head_count, frames, head_size), jnp.float32),
    )
    segment = lax.all_gather(kv_local, "frame", axis=0, tiled=True)
    segment_ids = ids_at(jnp.arange(segment.shape[0], dtype=jnp.int32), clip_ends)
    running_max, row_sum, weighted = fold_keys(
        initial, segment, segment_ids, queries_h, local_ids, clip_count
    )
    attn_exact = weighted / row_sum[..., None]
    log_total = running_max + jnp.log(row_sum)
    attention = join_heads(attn_exact).astype(jnp.bfloat16)
    branch_attn = jnp.dot(attention, w_ao, preferred_element_type=jnp.float32)
    after_attn = inputs + gate_attn * branch_attn * frame_valid
    normed_cross, inverse_cross = layer_norm(after_attn)
    cross_in = (normed_cross * gain_cross).astype(jnp.bfloat16)
    cross_queries = jnp.dot(cross_in, w_cq, preferred_element_type=jnp.float32).astype(jnp.bfloat16)
    text_rows = text_states[0].reshape(clip_count * text_slots, text_states.shape[3])
    text_kv = jnp.dot(text_rows, w_ckv, preferred_element_type=jnp.float32).astype(jnp.bfloat16)
    text_keys_h = split_heads(text_kv[:, :model_width], head_count)
    text_values_h = split_heads(text_kv[:, model_width:], head_count)
    slot_rows = jnp.arange(clip_count * text_slots, dtype=jnp.int32)
    text_clip = slot_rows // text_slots
    text_live = slot_rows % text_slots < jnp.repeat(text_len[0], text_slots)
    text_clip = jnp.where(text_live, text_clip, clip_count)
    cross_queries_h = split_heads(cross_queries, head_count)
    cross_scores = masked_scores(cross_queries_h, text_keys_h, text_clip, local_ids, clip_count)
    cross_probs = jax.nn.softmax(cross_scores, axis=-1)
    cross_low = cross_probs.astype(jnp.bfloat16)
    cross = join_heads(
        jnp.einsum("hqk,hkd->hqd", cross_low, text_values_h, preferred_element_type=jnp.float32)
    ).astype(jnp.bfloat16)
    branch_cross = jnp.dot(cross, w_co, preferred_element_type=jnp.float32)
    after_cross = after_attn + branch_cross * frame_valid
    normed_mlp, inverse_mlp = layer_norm(after_cross)
    mlp_in = (normed_mlp * (1.0 + scale_mlp) + shift_mlp).astype(jnp.bfloat16)
    hidden = jnp.dot(mlp_in, w_up, preferred_element_type=jnp.float32)
    activated, gelu_pull = jax.vjp(lambda value: jax.nn.gelu(value, approximate=True), hidden)
    activated = activated.astype(jnp.bfloat16)
    branch_mlp = jnp.dot(activated, w_down, preferred_element_type=jnp.float32)
    mixed = after_cross + gate_mlp * branch_mlp * frame_valid
    grad_out = cotangent[0].astype(jnp.float32)
    grad_mlp = (grad_out * gate_mlp * frame_valid).astype(jnp.bfloat16)
    grad_gate_mlp = grad_out * branch_mlp * frame_valid
    grad_w_down = jnp.dot(activated.T, grad_mlp, preferred_element_type=jnp.float32)
    grad_act = jnp.dot(grad_mlp, w_down.T, preferred_element_type=jnp.float32)
    grad_hidden = gelu_pull(grad_act)[0].astype(jnp.bfloat16)
    grad_w_up = jnp.dot(mlp_in.T, grad_hidden, preferred_element_type=jnp.float32)
    grad_mlp_in = jnp.dot(grad_hidden, w_up.T, preferred_element_type=jnp.float32)
    grad_cross_out = grad_out + norm_back(grad_mlp_in * (1.0 + scale_mlp), normed_mlp, inverse_mlp)
    grad_branch_cross = (grad_cross_out * frame_valid).astype(jnp.bfloat16)
    grad_w_co = jnp.dot(cross.T, grad_branch_cross, preferred_element_type=jnp.float32)
    grad_cross_h = split_heads(
        jnp.dot(grad_branch_cross, w_co.T, preferred_element_type=jnp.float32).astype(jnp.bfloat16),
        head_count,
    )
    cross_dprob = jnp.einsum(
        "hqd,hkd->hqk", grad_cross_h, text_values_h, preferred_element_type=jnp.float32
    )
    cross_dscore = (
        cross_probs * (cross_dprob - jnp.sum(cross_probs * cross_dprob, axis=-1, keepdims=True))
    ).astype(jnp.bfloat16)
    grad_cross_queries = (
        join_heads(
            jnp.einsum(
                "hqk,hkd->hqd", cross_dscore, text_keys_h, preferred_element_type=jnp.float32
            )
        )
        * score_scale
    ).astype(jnp.bfloat16)
    grad_text_keys = (
        join_heads(
            jnp.einsum(
                "hqk,hqd->hkd", cross_dscore, cross_queries_h, preferred_element_type=jnp.float32
            )
        )
        * score_scale
    )
    grad_text_values = join_heads(
        jnp.einsum("hqk,hqd->hkd", cross_low, grad_cross_h, preferred_element_type=jnp.float32)
    )
    grad_w_ckv = jnp.dot(
        text_rows.astype(jnp.float32).T,
        jnp.concatenate([grad_text_keys, grad_text_values], axis=1),
        precision=highest,
    )
    grad_w_cq = jnp.dot(cross_in.T, grad_cross_queries, preferred_element_type=jnp.float32)
    grad_cross_in = jnp.dot(grad_cross_queries, w_cq.T, preferred_element_type=jnp.float32)
    grad_gain_cross = jnp.sum(grad_cross_in * normed_cross, axis=0)
    grad_attn_out = grad_cross_out + norm_back(
        grad_cross_in * gain_cross, normed_cross, inverse_cross
    )
    grad_branch_attn = (grad_attn_out * gate_attn * frame_valid).astype(jnp.bfloat16)
    grad_gate_attn = grad_attn_out * branch_attn * frame_valid
    grad_w_ao = jnp.dot(attention.T, grad_branch_attn, preferred_element_type=jnp.float32)
    grad_attention_h = split_heads(
        jnp.dot(grad_branch_attn, w_ao.T, preferred_element_type=jnp.float32).astype(jnp.bfloat16),
        head_count,
    )
    delta = jnp.sum(grad_attention_h.astype(jnp.float32) * attn_exact, axis=-1)
    kv_all = lax.all_gather(kv_local, "frame", axis=0, tiled=True)
    all_ids = ids_at(jnp.arange(group_frames, dtype=jnp.int32), clip_ends)

    def score_grads(kv_block, id_block):
        keys_h = split_heads(kv_block[:, :model_width], head_count)
        values_h = split_heads(kv_block[:, model_width:], head_count)
        scores = masked_scores(queries_h, keys_h, id_block, local_ids, clip_count)
        probs = jnp.exp(scores - log_total[..., None])
        dprob = jnp.einsum(
            "hqd,hkd->hqk", grad_attention_h, values_h, preferred_element_type=jnp.float32
        )
        dscore = (probs * (dprob - delta[..., None])).astype(jnp.bfloat16)
        return (keys_h, probs, dscore)

    kv_blocks, id_blocks = split_blocks(kv_all, all_ids)

    def query_block(summed, element):
        keys_h, probs, dscore = score_grads(element[0], element[1])
        return (
            summed + jnp.einsum("hqk,hkd->hqd", dscore, keys_h, preferred_element_type=jnp.float32),
            None,
        )

    grad_queries_h = lax.scan(
        query_block, jnp.zeros((head_count, frames, head_size), jnp.float32), (kv_blocks, id_blocks)
    )[0]
    grad_queries = (join_heads(grad_queries_h) * score_scale).astype(jnp.bfloat16)
    key_ids = ids_at(jnp.arange(frames * lax.axis_size("frame"), dtype=jnp.int32), clip_ends)
    term_blocks, term_ids = split_blocks(kv_all, key_ids)

    def key_block(unused, element):
        keys_h, probs, dscore = score_grads(element[0], element[1])
        grad_keys_h = (
            jnp.einsum("hqk,hqd->hkd", dscore, queries_h, preferred_element_type=jnp.float32)
            * score_scale
        )
        grad_values_h = jnp.einsum(
            "hqk,hqd->hkd",
            probs.astype(jnp.bfloat16),
            grad_attention_h,
            preferred_element_type=jnp.float32,
        )
        return (
            unused,
            jnp.concatenate([join_heads(grad_keys_h), join_heads(grad_values_h)], axis=1),
        )

    stacked = lax.scan(key_block, jnp.zeros((), jnp.float32), (term_blocks, term_ids))[1]
    grad_kv = lax.psum_scatter(
        stacked.reshape(frames * lax.axis_size("frame"), 2 * model_width).astype(jnp.bfloat16),
        "frame",
        scatter_dimension=0,
        tiled=True,
    )
    grad_qkv = jnp.concatenate([grad_queries, grad_kv], axis=1)
    grad_w_qkv = jnp.dot(modulated.T, grad_qkv, preferred_element_type=jnp.float32)
    grad_mod_in = jnp.dot(grad_qkv, w_qkv.T, preferred_element_type=jnp.float32)
    grad_inputs = grad_attn_out + norm_back(
        grad_mod_in * (1.0 + scale_attn), normed_attn, inverse_attn
    )
    grad_frame_mod = jnp.concatenate(
        [
            grad_mod_in,
            grad_mod_in * normed_attn,
            grad_gate_attn,
            grad_mlp_in,
            grad_mlp_in * normed_mlp,
            grad_gate_mlp,
        ],
        axis=1,
    )
    grad_modulation = jnp.dot(onehot.T, grad_frame_mod, precision=highest)
    grad_w_ada = jnp.dot(time_low.astype(jnp.float32).T, grad_modulation, precision=highest)
    grad_b_ada = jnp.sum(grad_modulation, axis=0)
    (
        grad_w_ada,
        grad_b_ada,
        grad_w_qkv,
        grad_w_ao,
        grad_gain_cross,
        grad_w_cq,
        grad_w_ckv,
        grad_w_co,
        grad_w_up,
        grad_w_down,
    ) = lax.psum(
        (
            grad_w_ada,
            grad_b_ada,
            grad_w_qkv,
            grad_w_ao,
            grad_gain_cross,
            grad_w_cq,
            grad_w_ckv,
            grad_w_co,
            grad_w_up,
            grad_w_down,
        ),
        ("batch", "frame"),
    )
    return (
        mixed.astype(jnp.bfloat16)[None],
        grad_inputs.astype(jnp.bfloat16)[None],
        grad_w_ada,
        grad_b_ada,
        grad_w_qkv,
        grad_w_ao,
        grad_gain_cross,
        grad_w_cq,
        grad_w_ckv,
        grad_w_co,
        grad_w_up,
        grad_w_down,
    )


def solution(mesh):
    placed = (
        P("batch", "frame", None),
        P("batch", None, None),
        P("batch", None, None, None),
        P("batch", None),
        P("batch", None),
        P("batch", "frame", None),
        P(),
        P(),
        P(),
        P(),
        P(),
        P(),
        P(),
        P(),
        P(),
        P(),
    )
    return jax.shard_map(
        per_device,
        mesh=mesh,
        in_specs=placed,
        out_specs=(
            P("batch", "frame", None),
            P("batch", "frame", None),
            P(),
            P(),
            P(),
            P(),
            P(),
            P(),
            P(),
            P(),
            P(),
            P(),
        ),
        check_vma=False,
    )
```

profile of v0, /device:TPU:0, one launch (start us, length us, event | category | flops | bytes accessed | tf_op | source)
XLA Modules:
  0.0 769.2 jit_solution(16924569171686367964)
XLA Ops:
  11.9 2.0 fusion.104
  14.0 2.1 copy-done.5
  19.2 1.9 convolution_convert_fusion.1
  24.0 96.0 %all-gather.2.cloned.1.call-done = bf16[4096,768]{1,0:T(8,128)(2,1)} async-done(((bf16[512,768]{1,0:T(8,128)(2,1)}), bf16[4096,768]{1,0:T(8,128)(2,1)}) %all-gather.2.cloned.1.call-update) | async-done | bytes 6291472 | tf_op jit(solution)/shard_map/all_gather | solution.py:139
  120.0 8.7 %copy.97 = bf16[4,1024,768]{1,2,0:T(8,128)(2,1)} copy(bf16[4,1024,768]{2,1,0:T(8,128)(2,1)} %bitcast.337) | data formatting | bytes 12582912
  128.7 86.6 %while.37 = (s32[]{:T(128)}, f32[6,512]{1,0:T(8,128)S(1)}, f32[6,512]{1,0:T(8,128)S(1)}, f32[6,512,64]{1,2,0:T(8,128)}, s32[512]{0:T(512)S(1)}, /*index=5*/s32[4...) while((s32[]{:T(128)}, f32[6,512]{1,0:T(8,128)S(1)}, ...), condition=%wide.region_8.9_spmd.clone, body=%wide.region_5.8_spmd.clone.sunk | while | flops 841564160 | bytes 106512592 | solution.py:86
  131.3 6.7 fusion.255
  138.0 7.3 fusion.256
  146.2 3.3 fusion.258
  152.9 6.7 fusion.255
  159.6 7.3 fusion.256
  167.8 3.3 fusion.258
  174.5 6.7 fusion.255
  181.2 7.3 fusion.256
  189.4 3.3 fusion.258
  196.1 6.7 fusion.255
  202.8 7.3 fusion.256
  211.0 3.3 fusion.258
  216.6 3.3 fusion.129
  220.8 6.1 fusion.136
  226.9 3.6 fusion.69
  233.6 2.8 fusion.52
  241.4 3.7 multiply_reduce_fusion
  245.2 4.5 multiply_convert_fusion
  255.8 117.5 %while.36 = (s32[]{:T(128)}, bf16[4,1024,768]{2,1,0:T(8,128)(2,1)}, s32[512]{0:T(512)S(1)}, s32[4,1024]{1,0:T(4,128)S(1)}, bf16[4,1024,768]{1,2,0:T(8,128)(2,1)}...) while((s32[]{:T(128)}, bf16[4,1024,768]{2,1,0:T(8,128)(2,1)}, ...), condition=%wide.region_24.25_spmd, body=%wide.region_23.24_spmd.sunk | while | flops 1647051776 | bytes 62968484 | solution.py:282
  258.7 6.4 fusion.247
  265.0 10.4 %fusion.249 = bf16[6,1024,64]{1,2,0:T(8,128)(2,1)S(1)} fusion(bf16[6,512,64]{1,2,0:T(8,128)(2,1)S(1)} %get-tuple-element.687, f32[6,1024,512]{2,1,0:T(8,128)} %fusion.247, f32[6,512]{1,0:T(8,128)S(1)} %get-tuple-element.690, f32[6,512]{1,0:T(8,128)S(1)} %get-tuple-element.688, pred[512,1024]{0,1:T(8,128)(4,1)S(1)} %compare_and_fusion.7, ...), kind=kOutput, calls=%fused_computation.14.clone.1 | convolution fusion | flops 824967168 | bytes 15491072 | tf_op jit(solution)/shard_map/while/body/eval_jaxpr/hqk,hqd->hkd/dot_general | solution.py:268
  275.5 7.8 %fusion.248 = bf16[6,1024,64]{1,2,0:T(8,128)(2,1)S(1)} fusion(bf16[6,512,64]{1,2,0:T(8,128)(2,1)} %get-tuple-element.689, f32[6,1024,512]{2,1,0:T(8,128)} %fusion.247, f32[6,512]{1,0:T(8,128)S(1)} %get-tuple-element.688, pred[512,1024]{0,1:T(8,128)(4,1)S(1)} %compare_and_fusion.7), kind=kOutput, calls=%fused_computation.6.clone.1 | convolution fusion | flops 415236096 | bytes 14299136 | tf_op jit(solution)/shard_map/while/body/eval_jaxpr/hqk,hqd->hkd/dot_general | solution.py:271
  288.0 6.4 fusion.247
  294.3 10.4 %fusion.249 = bf16[6,1024,64]{1,2,0:T(8,128)(2,1)S(1)} fusion(bf16[6,512,64]{1,2,0:T(8,128)(2,1)S(1)} %get-tuple-element.687, f32[6,1024,512]{2,1,0:T(8,128)} %fusion.247, f32[6,512]{1,0:T(8,128)S(1)} %get-tuple-element.690, f32[6,512]{1,0:T(8,128)S(1)} %get-tuple-element.688, pred[512,1024]{0,1:T(8,128)(4,1)S(1)} %compare_and_fusion.7, ...), kind=kOutput, calls=%fused_computation.14.clone.1 | convolution fusion | flops 824967168 | bytes 15491072 | tf_op jit(solution)/shard_map/while/body/eval_jaxpr/hqk,hqd->hkd/dot_general | solution.py:268
  304.8 7.8 %fusion.248 = bf16[6,1024,64]{1,2,0:T(8,128)(2,1)S(1)} fusion(bf16[6,512,64]{1,2,0:T(8,128)(2,1)} %get-tuple-element.689, f32[6,1024,512]{2,1,0:T(8,128)} %fusion.247, f32[6,512]{1,0:T(8,128)S(1)} %get-tuple-element.688, pred[512,1024]{0,1:T(8,128)(4,1)S(1)} %compare_and_fusion.7), kind=kOutput, calls=%fused_computation.6.clone.1 | convolution fusion | flops 415236096 | bytes 14299136 | tf_op jit(solution)/shard_map/while/body/eval_jaxpr/hqk,hqd->hkd/dot_general | solution.py:271
  317.2 6.4 fusion.247
  323.6 10.4 %fusion.249 = bf16[6,1024,64]{1,2,0:T(8,128)(2,1)S(1)} fusion(bf16[6,512,64]{1,2,0:T(8,128)(2,1)S(1)} %get-tuple-element.687, f32[6,1024,512]{2,1,0:T(8,128)} %fusion.247, f32[6,512]{1,0:T(8,128)S(1)} %get-tuple-element.690, f32[6,512]{1,0:T(8,128)S(1)} %get-tuple-element.688, pred[512,1024]{0,1:T(8,128)(4,1)S(1)} %compare_and_fusion.7, ...), kind=kOutput, calls=%fused_computation.14.clone.1 | convolution fusion | flops 824967168 | bytes 15491072 | tf_op jit(solution)/shard_map/while/body/eval_jaxpr/hqk,hqd->hkd/dot_general | solution.py:268
  334.0 7.8 %fusion.248 = bf16[6,1024,64]{1,2,0:T(8,128)(2,1)S(1)} fusion(bf16[6,512,64]{1,2,0:T(8,128)(2,1)} %get-tuple-element.689, f32[6,1024,512]{2,1,0:T(8,128)} %fusion.247, f32[6,512]{1,0:T(8,128)S(1)} %get-tuple-element.688, pred[512,1024]{0,1:T(8,128)(4,1)S(1)} %compare_and_fusion.7), kind=kOutput, calls=%fused_computation.6.clone.1 | convolution fusion | flops 415236096 | bytes 14299136 | tf_op jit(solution)/shard_map/while/body/eval_jaxpr/hqk,hqd->hkd/dot_general | solution.py:271
  346.6 6.4 fusion.247
  353.0 10.4 %fusion.249 = bf16[6,1024,64]{1,2,0:T(8,128)(2,1)S(1)} fusion(bf16[6,512,64]{1,2,0:T(8,128)(2,1)S(1)} %get-tuple-element.687, f32[6,1024,512]{2,1,0:T(8,128)} %fusion.247, f32[6,512]{1,0:T(8,128)S(1)} %get-tuple-element.690, f32[6,512]{1,0:T(8,128)S(1)} %get-tuple-element.688, pred[512,1024]{0,1:T(8,128)(4,1)S(1)} %compare_and_fusion.7, ...), kind=kOutput, calls=%fused_computation.14.clone.1 | convolution fusion | flops 824967168 | bytes 15491072 | tf_op jit(solution)/shard_map/while/body/eval_jaxpr/hqk,hqd->hkd/dot_general | solution.py:268
  363.4 7.8 %fusion.248 = bf16[6,1024,64]{1,2,0:T(8,128)(2,1)S(1)} fusion(bf16[6,512,64]{1,2,0:T(8,128)(2,1)} %get-tuple-element.689, f32[6,1024,512]{2,1,0:T(8,128)} %fusion.247, f32[6,512]{1,0:T(8,128)S(1)} %get-tuple-element.688, pred[512,1024]{0,1:T(8,128)(4,1)S(1)} %compare_and_fusion.7), kind=kOutput, calls=%fused_computation.6.clone.1 | convolution fusion | flops 415236096 | bytes 14299136 | tf_op jit(solution)/shard_map/while/body/eval_jaxpr/hqk,hqd->hkd/dot_general | solution.py:271
  373.4 84.4 %while.38 = (s32[]{:T(128)}, f32[6,512,64]{1,2,0:T(8,128)}, s32[512]{0:T(512)S(1)}, s32[4,1024]{1,0:T(4,128)S(1)}, bf16[4,1024,768]{1,2,0:T(8,128)(2,1)}, /*inde...) while((s32[]{:T(128)}, f32[6,512,64]{1,2,0:T(8,128)}, ...), condition=%wide.region_22.23_spmd.clone, body=%wide.region_21.22_spmd.clone.sunk | while | flops 1228276736 | bytes 46702800 | solution.py:258
  377.3 6.4 fusion.266
  383.7 10.1 %fusion.267 = f32[6,512,64]{1,2,0:T(8,128)S(1)} fusion(bf16[6,1024,64]{1,2,0:T(8,128)(2,1)S(1)} %bitcast.326, f32[6,1024,512]{2,1,0:T(8,128)} %fusion.266, f32[6,512]{1,0:T(8,128)S(1)} %get-tuple-element.722, f32[6,512]{1,0:T(8,128)S(1)} %get-tuple-element.720, pred[512,1024]{0,1:T(8,128)(4,1)S(1)} %compare_and_fusion.9, ...), kind=kOutput, calls=%fused_computation.51.clone.1 | convolution fusion | flops 824573952 | bytes 16670721 | tf_op jit(solution)/shard_map/while/body/eval_jaxpr/hqk,hkd->hqd/dot_general | solution.py:254
  395.6 1.6 dynamic-slice_bitcast_fusion.8
  398.2 6.4 fusion.266
  404.5 10.4 %fusion.267 = f32[6,512,64]{1,2,0:T(8,128)S(1)} fusion(bf16[6,1024,64]{1,2,0:T(8,128)(2,1)S(1)} %bitcast.326, f32[6,1024,512]{2,1,0:T(8,128)} %fusion.266, f32[6,512]{1,0:T(8,128)S(1)} %get-tuple-element.722, f32[6,512]{1,0:T(8,128)S(1)} %get-tuple-element.720, pred[512,1024]{0,1:T(8,128)(4,1)S(1)} %compare_and_fusion.9, ...), kind=kOutput, calls=%fused_computation.51.clone.1 | convolution fusion | flops 824573952 | bytes 16670721 | tf_op jit(solution)/shard_map/while/body/eval_jaxpr/hqk,hkd->hqd/dot_general | solution.py:254
  416.7 1.6 dynamic-slice_bitcast_fusion.8
  419.3 6.4 fusion.266
  425.7 10.3 %fusion.267 = f32[6,512,64]{1,2,0:T(8,128)S(1)} fusion(bf16[6,1024,64]{1,2,0:T(8,128)(2,1)S(1)} %bitcast.326, f32[6,1024,512]{2,1,0:T(8,128)} %fusion.266, f32[6,512]{1,0:T(8,128)S(1)} %get-tuple-element.722, f32[6,512]{1,0:T(8,128)S(1)} %get-tuple-element.720, pred[512,1024]{0,1:T(8,128)(4,1)S(1)} %compare_and_fusion.9, ...), kind=kOutput, calls=%fused_computation.51.clone.1 | convolution fusion | flops 824573952 | bytes 16670721 | tf_op jit(solution)/shard_map/while/body/eval_jaxpr/hqk,hkd->hqd/dot_general | solution.py:254
  440.3 6.4 fusion.266
  446.7 10.1 %fusion.267 = f32[6,512,64]{1,2,0:T(8,128)S(1)} fusion(bf16[6,1024,64]{1,2,0:T(8,128)(2,1)S(1)} %bitcast.326, f32[6,1024,512]{2,1,0:T(8,128)} %fusion.266, f32[6,512]{1,0:T(8,128)S(1)} %get-tuple-element.722, f32[6,512]{1,0:T(8,128)S(1)} %get-tuple-element.720, pred[512,1024]{0,1:T(8,128)(4,1)S(1)} %compare_and_fusion.9, ...), kind=kOutput, calls=%fused_computation.51.clone.1 | convolution fusion | flops 824573952 | bytes 16670721 | tf_op jit(solution)/shard_map/while/body/eval_jaxpr/hqk,hkd->hqd/dot_general | solution.py:254
  459.4 2.7 fusion.142
  463.4 2.5 fusion.128
  467.0 3.9 fusion.60
  471.0 2.5 fusion.64
  473.5 2.2 fusion.143
  475.8 2.4 fusion.144
  478.2 11.5 %reduce-scatter.2.cloned.1.call-done = bf16[512,768]{1,0:T(8,128)(2,1)} async-done(((bf16[4096,768]{1,0:T(8,128)(2,1)}), bf16[512,768]{1,0:T(8,128)(2,1)}) %reduce-scatter.2.cloned.1.call-update) | async-done | bytes 786448 | tf_op jit(solution)/shard_map/reduce_scatter | solution.py:283
  489.7 2.7 fusion.127
  492.4 2.4 fusion.87
  496.3 1.7 fusion.138
  498.0 3.4 fusion.122
  501.4 1.9 fusion.94
  504.0 41.3 %all-reduce = (f32[2304]{0:T(1024)}, f32[384]{0:T(512)}) all-reduce(f32[2304]{0:T(1024)S(1)} %get-tuple-element.437, f32[384]{0:T(512)S(1)} %copy-done.84), channel_id=1, replica_groups=mesh['batch'=4,'frame'=8] {'batch','frame'}, use_global_device_ids=true, to_apply=%region_30.31 | all-reduce | flops 2688 | bytes 21504 | tf_op jit(solution)/shard_map/psum | solution.py:320
  545.3 203.5 %all-reduce.4.cloned.1.call-done = (f32[384,2304]{1,0:T(8,128)}, f32[384,1152]{1,0:T(8,128)}, f32[384,384]{1,0:T(8,128)}, f32[384,384]{1,0:T(8,128)}, f32[512,76...) async-done(((f32[384,2304]{1,0:T(8,128)}, f32[384,1152]{1,0:T(8,128)}, f32[384,384]{1,0:T(8,128)}, f32[384,384]{1,0:T(8,128)}, ...) | async-done | bytes 13369360 | tf_op jit(solution)/shard_map/psum | solution.py:320
  748.8 3.0 copy.121
  751.8 4.2 copy.195
  (375 shorter events, 88.6 us)
Async XLA Ops:
  7.2 112.8 %all-gather.2.cloned.1.call-start = ((), (), s32[]{:S(2)}) async-start(), calls=%async_computation.1 | async-start | bytes 7077888 | tf_op jit(solution)/shard_map/all_gather | solution.py:139
  8.5 5.4 copy-start.75
  9.8 4.1 copy-start.79
  10.7 5.3 copy-start.15
  11.9 4.5 copy-start.51
  18.2 471.5 %reduce-scatter.2.cloned.1.call-start = ((), (), s32[]{:S(2)}) async-start(), calls=%async_computation.2 | async-start | bytes 7077888 | tf_op jit(solution)/shard_map/reduce_scatter | solution.py:283
  18.8 4.2 copy-start.85
  23.1 229.0 %copy-start.65 = (f32[512]{0:T(512)}, f32[512]{0:T(512)S(1)}, u32[]{:S(2)}) copy-start(f32[512]{0:T(512)S(1)} %compare_convert_fusion) | copy-start | bytes 6148
  131.3 14.1 %copy-start.31 = (f32[6,512,64]{1,2,0:T(8,128)S(1)}, f32[6,512,64]{1,2,0:T(8,128)}, u32[]{:S(2)}) copy-start(f32[6,512,64]{1,2,0:T(8,128)} %get-tuple-element.645) | copy-start | bytes 2359300 | tf_op jit(solution)/shard_map/while
  138.0 8.2 %copy-start.2 = (f32[6,1024,512]{2,1,0:T(8,128)S(1)}, f32[6,1024,512]{2,1,0:T(8,128)}, u32[]{:S(2)}) copy-start(f32[6,1024,512]{2,1,0:T(8,128)} %get-tuple-element.615) | copy-start | bytes 37748740 | tf_op jit(solution)/shard_map/while
  152.9 14.1 %copy-start.31 = (f32[6,512,64]{1,2,0:T(8,128)S(1)}, f32[6,512,64]{1,2,0:T(8,128)}, u32[]{:S(2)}) copy-start(f32[6,512,64]{1,2,0:T(8,128)} %get-tuple-element.645) | copy-start | bytes 2359300 | tf_op jit(solution)/shard_map/while
  159.6 8.2 %copy-start.2 = (f32[6,1024,512]{2,1,0:T(8,128)S(1)}, f32[6,1024,512]{2,1,0:T(8,128)}, u32[]{:S(2)}) copy-start(f32[6,1024,512]{2,1,0:T(8,128)} %get-tuple-element.615) | copy-start | bytes 37748740 | tf_op jit(solution)/shard_map/while
  174.5 14.1 %copy-start.31 = (f32[6,512,64]{1,2,0:T(8,128)S(1)}, f32[6,512,64]{1,2,0:T(8,128)}, u32[]{:S(2)}) copy-start(f32[6,512,64]{1,2,0:T(8,128)} %get-tuple-element.645) | copy-start | bytes 2359300 | tf_op jit(solution)/shard_map/while
  181.2 8.2 %copy-start.2 = (f32[6,1024,512]{2,1,0:T(8,128)S(1)}, f32[6,1024,512]{2,1,0:T(8,128)}, u32[]{:S(2)}) copy-start(f32[6,1024,512]{2,1,0:T(8,128)} %get-tuple-element.615) | copy-start | bytes 37748740 | tf_op jit(solution)/shard_map/while
  196.1 14.1 %copy-start.31 = (f32[6,512,64]{1,2,0:T(8,128)S(1)}, f32[6,512,64]{1,2,0:T(8,128)}, u32[]{:S(2)}) copy-start(f32[6,512,64]{1,2,0:T(8,128)} %get-tuple-element.645) | copy-start | bytes 2359300 | tf_op jit(solution)/shard_map/while
  202.8 8.2 %copy-start.2 = (f32[6,1024,512]{2,1,0:T(8,128)S(1)}, f32[6,1024,512]{2,1,0:T(8,128)}, u32[]{:S(2)}) copy-start(f32[6,1024,512]{2,1,0:T(8,128)} %get-tuple-element.615) | copy-start | bytes 37748740 | tf_op jit(solution)/shard_map/while
  215.3 4.9 copy-start.63
  215.3 4.9 copy-start.77
  216.6 4.2 copy-start.26
  216.6 4.2 copy-start.47
  219.9 13.7 %copy-start.45 = (bf16[512,384]{1,0:T(8,128)(2,1)}, bf16[512,384]{1,0:T(8,128)(2,1)S(1)}, u32[]{:S(2)}) copy-start(bf16[512,384]{1,0:T(8,128)(2,1)S(1)} %get-tuple-element.419) | copy-start | bytes 1179652
  219.9 32.2 %copy-start.6 = (f32[512,384]{1,0:T(8,128)}, f32[512,384]{1,0:T(8,128)S(1)}, u32[]{:S(2)}) copy-start(f32[512,384]{1,0:T(8,128)S(1)} %get-tuple-element.406) | copy-start | bytes 2359300
  219.9 32.2 %copy-start.69 = (f32[512]{0:T(512)}, f32[512]{0:T(512)S(1)}, u32[]{:S(2)}) copy-start(f32[512]{0:T(512)S(1)} %broadcast_multiply_fusion.7) | copy-start | bytes 6148
  220.2 32.0 %copy-start.73 = (f32[512]{0:T(512)}, f32[512]{0:T(512)S(1)}, u32[]{:S(2)}) copy-start(f32[512]{0:T(512)S(1)} %add_rsqrt_fusion.1) | copy-start | bytes 6148
  220.8 6.2 copy-start.39
  220.8 6.1 copy-start.59
  220.8 10.6 %slice-start = ((s8[4718592]{0:T(1024)(128)(4,1)}), s8[524288]{0:T(1024)(128)(4,1)S(1)}, s32[]{:S(2)}) async-start(s8[4718592]{0:T(1024)(128)(4,1)} %bitcast.329), calls=%async_computation.4 | async-start | bytes 1048576
  226.9 18.2 %copy-start.81 = (f32[6,512]{1,0:T(8,128)}, f32[6,512]{1,0:T(8,128)S(1)}, u32[]{:S(2)}) copy-start(f32[6,512]{1,0:T(8,128)S(1)} %get-tuple-element.426) | copy-start | bytes 36868
  226.9 4.5 slice-start.1
  231.1 7.4 copy-start.10
  231.1 7.4 copy-start.67
  231.4 7.1 copy-start.71
  236.4 5.0 slice-start.2
  240.9 11.3 %copy-start.13 = (f32[512,384]{1,0:T(8,128)}, f32[512,384]{1,0:T(8,128)S(1)}, u32[]{:S(2)}) copy-start(f32[512,384]{1,0:T(8,128)S(1)} %get-tuple-element.417) | copy-start | bytes 2359300
  256.1 8.9 %copy-start.3 = (bf16[6,512,64]{1,2,0:T(8,128)(2,1)}, bf16[6,512,64]{1,2,0:T(8,128)(2,1)S(1)}, u32[]{:S(2)}) copy-start(bf16[6,512,64]{1,2,0:T(8,128)(2,1)S(1)} %get-tuple-element.687) | copy-start | bytes 1179652 | tf_op jit(solution)/shard_map/while
  285.4 8.9 %copy-start.3 = (bf16[6,512,64]{1,2,0:T(8,128)(2,1)}, bf16[6,512,64]{1,2,0:T(8,128)(2,1)S(1)}, u32[]{:S(2)}) copy-start(bf16[6,512,64]{1,2,0:T(8,128)(2,1)S(1)} %get-tuple-element.687) | copy-start | bytes 1179652 | tf_op jit(solution)/shard_map/while
  314.7 8.9 %copy-start.3 = (bf16[6,512,64]{1,2,0:T(8,128)(2,1)}, bf16[6,512,64]{1,2,0:T(8,128)(2,1)S(1)}, u32[]{:S(2)}) copy-start(bf16[6,512,64]{1,2,0:T(8,128)(2,1)S(1)} %get-tuple-element.687) | copy-start | bytes 1179652 | tf_op jit(solution)/shard_map/while
  344.1 8.9 %copy-start.3 = (bf16[6,512,64]{1,2,0:T(8,128)(2,1)}, bf16[6,512,64]{1,2,0:T(8,128)(2,1)S(1)}, u32[]{:S(2)}) copy-start(bf16[6,512,64]{1,2,0:T(8,128)(2,1)S(1)} %get-tuple-element.687) | copy-start | bytes 1179652 | tf_op jit(solution)/shard_map/while
  373.4 375.4 %all-reduce.4.cloned.1.call-start = ((), (), s32[]{:S(2)}) async-start(), calls=%async_computation.3 | async-start | bytes 26738688 | tf_op jit(solution)/shard_map/psum | solution.py:320
  377.3 6.4 copy-start.12
  377.3 6.4 copy-start.52
  398.2 6.4 copy-start.12
  398.2 6.4 copy-start.52
  419.3 6.4 copy-start.12
  419.3 6.4 copy-start.52
  440.3 6.4 copy-start.12
  440.3 6.4 copy-start.52
  457.8 4.3 copy-start.14
  457.8 4.3 copy-start.44
  457.8 4.3 copy-start.66
  457.8 5.6 copy-start.7
  457.8 5.5 copy-start.70
  457.8 5.5 copy-start.74
  457.8 5.5 copy-start.78
  459.2 6.7 copy-start.40
  459.4 6.5 copy-start.9
  475.7 13.9 %copy-start.16 = (bf16[1,512,384]{2,1,0:T(8,128)(2,1)S(1)}, bf16[1,512,384]{2,1,0:T(8,128)(2,1)}, u32[]{:S(2)}) copy-start(bf16[1,512,384]{2,1,0:T(8,128)(2,1)} %param.22) | copy-start | bytes 1179652
  475.7 13.9 %copy-start.76 = (f32[512]{0:T(512)S(1)}, f32[512]{0:T(512)}, u32[]{:S(2)}) copy-start(f32[512]{0:T(512)} %copy-done.75) | copy-start | bytes 6148
  475.7 13.9 %copy-start.80 = (f32[512]{0:T(512)S(1)}, f32[512]{0:T(512)}, u32[]{:S(2)}) copy-start(f32[512]{0:T(512)} %copy-done.79) | copy-start | bytes 6148
  478.2 14.2 %copy-start.19 = (f32[512,384]{1,0:T(8,128)S(1)}, f32[512,384]{1,0:T(8,128)}, u32[]{:S(2)}) copy-start(f32[512,384]{1,0:T(8,128)} %get-tuple-element.404) | copy-start | bytes 2359300
  496.3 5.2 copy-start.23
  496.3 5.1 copy-start.54
  751.8 4.2 copy-start.38
  751.8 5.4 copy-start.57
  (55 other events, 120.5 us)
Sparse Core Ops, SparseCore 0:
  18.3 101.7 all-gather.1
  373.5 116.1 reduce-scatter.1
  503.5 245.2 all-reduce.3
where the time goes:
time: 774 us; the launch traced here: 769 us
  waiting for transfers between devices  311 us (40%)
  matrix products  267 us (34%)
  local copies, waits for them, and re-layouts  73.2 us (9%)
  other arithmetic  59.7 us (8%)
  blocking collectives  41.3 us (5%)
  between operations  15.1 us (2%)
    psum x1, waiting for transfers between devices, per_device(): lax.psum((grad_w_ada, grad_b_ada, grad_w_qkv, grad_w_ao, grad_gain_cross,...  203 us
    all_gather x1, waiting for transfers between devices, per_device(): segment = lax.all_gather(kv_local, 'frame', axis=0, tiled=True)  96 us
    dot_general x12, matrix products, masked_scores(): jnp.einsum('hqd,hkd->hqk', queries_h, keys_h, preferred_element_type=jnp....  78 us
    dot_general x4, matrix products, key_block(): jnp.einsum('hqk,hqd->hkd', dscore, queries_h, preferred_element_type=jnp....  41.7 us
    psum x1, blocking collectives, per_device(): lax.psum((grad_w_ada, grad_b_ada, grad_w_qkv, grad_w_ao, grad_gain_cross,...  41.3 us
    dot_general x4, matrix products, query_block(): jnp.einsum('hqk,hkd->hqd', dscore, keys_h, preferred_element_type=jnp.flo...  40.9 us
    dot_general x4, matrix products, key_block(): jnp.einsum('hqk,hqd->hkd', probs.astype(jnp.bfloat16), grad_attention_h,...  31.3 us
    reduce_sum x4, other arithmetic, per_block(): row_sum = row_sum * factor + jnp.sum(weights_now, axis=-1)  29.3 us
  transfers between devices with their start and end apart: 3, of which 3 were waited for; matrix products, arithmetic and copies ran while one was open for 14% of the time, Pallas kernels for 0%

commit v1 on v0

v1 whole, which is shorter than its diff:
```python
import functools

import jax
import jax.numpy as jnp
from jax import lax
from jax.experimental import pallas as pl
from jax.experimental.pallas import tpu as pltpu
from jax.sharding import PartitionSpec as P

HEADS = 6
LANES = 128
MASKED = -1e30

f32 = jnp.float32
bf16 = jnp.bfloat16
highest = lax.Precision.HIGHEST
eps_norm = 1e-06
MESH = pl.DeviceIdType.MESH

NT = (((1,), (1,)), ((), ()))
NN = (((1,), (0,)), ((), ()))
TN = (((0,), (0,)), ((), ()))


def dg(left, right, dims):
    return lax.dot_general(left, right, dims, preferred_element_type=f32)


def layer_norm(values):
    center = values - jnp.mean(values, axis=-1, keepdims=True)
    inverse = lax.rsqrt(jnp.mean(center * center, axis=-1, keepdims=True) + eps_norm)
    return (center * inverse, inverse)


def norm_back(grad, normed, inverse):
    mean_grad = jnp.mean(grad, axis=-1, keepdims=True)
    mean_prod = jnp.mean(grad * normed, axis=-1, keepdims=True)
    return (grad - mean_grad - normed * mean_prod) * inverse


def pieces(value):
    high = value.astype(bf16)
    rest = value - high.astype(f32)
    middle = rest.astype(bf16)
    low = (rest - middle.astype(f32)).astype(bf16)
    return high, middle, low


def nearest(step, me, count):
    lower = me < count // 2
    mine = jnp.where(lower, me, count - 1 - me)
    index = jnp.where(step - 1 < mine, step - 1, step)
    return jnp.where(lower, index, count - 1 - index)


def place():
    batch = lax.axis_index("batch")
    frame = lax.axis_index("frame")
    side = lax.rem(frame, 2)
    column = lax.div(frame, 2)
    return batch, frame, side, column, frame + 1 - 2 * side


def greet(batch, side, column, count, peer):
    barrier = pltpu.get_barrier_semaphore()
    pl.semaphore_signal(barrier, inc=1, device_id=(batch, peer), device_id_type=MESH)
    for step in range(1, count):
        other = nearest(step, column, count)
        pl.semaphore_signal(
            barrier, inc=1, device_id=(batch, 2 * other + side), device_id_type=MESH
        )
    pl.semaphore_wait(barrier, count)


def forward_kernel(
    frames,
    count,
    mod_own,
    w_qp,
    w_kp,
    w_vp,
    key_aug,
    query_aug,
    attention,
    stats,
    mod_all,
    mod_peer,
    pairs,
    queries,
    total,
    tops,
    part_out,
    part_in,
    stat_out,
    stat_in,
    send_sem,
    recv_sem,
):
    batch, frame, side, column, peer = place()
    head_size = mod_own.shape[1] // HEADS
    greet(batch, side, column, count, peer)

    def to_peer(source, target, slot):
        return pltpu.make_async_remote_copy(
            src_ref=source,
            dst_ref=target,
            send_sem=send_sem.at[slot],
            recv_sem=recv_sem.at[slot],
            device_id=(batch, peer),
            device_id_type=MESH,
        )

    def to_column(step, other, slot):
        return pltpu.make_async_remote_copy(
            src_ref=mod_own,
            dst_ref=mod_all.at[slot],
            send_sem=send_sem.at[2 + step],
            recv_sem=recv_sem.at[3 + slot],
            device_id=(batch, 2 * other + side),
            device_id_type=MESH,
        )

    swap = to_peer(mod_own, mod_peer, 0)
    sends = [
        to_column(step, nearest(step, column, count), column) for step in range(1, count)
    ]
    for index, send in enumerate(sends):
        send.start()
        if index == 0:
            swap.start()
    mod_all[column] = mod_own[...]
    total[...] = jnp.zeros_like(total)
    tops[...] = jnp.full_like(tops, -1e38)
    ones = (lax.broadcasted_iota(jnp.int32, (frames, LANES), 1) >= head_size).astype(bf16)

    def make_queries(half, source):
        rows = pl.ds(half * frames, frames)
        flat = dg(source, w_qp[...], NN).astype(bf16)
        extra = query_aug[rows, :]
        for head in range(HEADS):
            queries[head, rows, :] = flat[:, head * LANES : (head + 1) * LANES] * 0.125 + extra

    def make_keys(block):
        source = mod_all[block]
        flat = dg(source, w_kp[...], NN).astype(bf16)
        extra = key_aug[block]
        for head in range(HEADS):
            pairs[block, 0, head] = flat[:, head * LANES : (head + 1) * LANES] + extra
        flat = dg(source, w_vp[...], NN).astype(bf16)
        for head in range(HEADS):
            pairs[block, 1, head] = flat[:, head * LANES : (head + 1) * LANES] + ones

    def attend(half, block):
        rows = pl.ds(half * frames, frames)

        def scores(head):
            now = dg(pairs[block, 0, head], queries[head, rows, :], NT)
            return now, jnp.max(now, axis=0, keepdims=True)

        ahead = scores(0)
        for head in range(HEADS):
            now, top = ahead
            if head + 1 < HEADS:
                ahead = scores(head + 1)
            before = tops[head, :1, rows]
            new = jnp.maximum(before, top)
            probs = jnp.exp(now - new).astype(bf16)
            total[head, :, rows] = total[head, :, rows] * jnp.exp(before - new) + dg(
                pairs[block, 1, head], probs, TN
            )
            tops[head, :, rows] = jnp.broadcast_to(new, (8, frames))

    def arrive(step):
        block = nearest(step, column, count)
        to_column(step, block, block).wait_recv()
        make_keys(block)
        return block

    make_queries(0, mod_own[...])
    make_keys(column)
    attend(0, column)
    swap.wait()
    make_queries(1, mod_peer[...])
    attend(1, column)

    def per_block(step, unused):
        block = arrive(step)
        attend(0, block)
        attend(1, block)
        return unused

    lax.fori_loop(1, count - 1, per_block, 0)
    block = arrive(count - 1)
    attend(1, block)
    there = pl.ds(frames, frames)
    for head in range(HEADS):
        part_out[head * head_size : (head + 1) * head_size, :] = total[
            head, :head_size, there
        ].astype(bf16)
        stat_out[head : head + 1, :] = tops[head, :1, there]
        stat_out[8 + head : 9 + head, :] = total[head, head_size : head_size + 1, there]
    parts = to_peer(part_out, part_in, 1)
    numbers = to_peer(stat_out, stat_in, 2)
    numbers.start()
    parts.start()
    attend(0, block)
    numbers.wait()
    parts.wait()
    here = pl.ds(0, frames)
    joined = []
    logs = []
    for head in range(HEADS):
        mine, theirs = tops[head, :1, here], stat_in[head : head + 1, :]
        new = jnp.maximum(mine, theirs)
        left, right = jnp.exp(mine - new), jnp.exp(theirs - new)
        row_sum = (
            total[head, head_size : head_size + 1, here] * left
            + stat_in[8 + head : 9 + head, :] * right
        )
        logs.append(new + jnp.log(row_sum))
        scale = 1.0 / row_sum
        joined.append(
            total[head, :head_size, here] * (left * scale)
            + part_in[head * head_size : (head + 1) * head_size, :].astype(f32) * (right * scale)
        )
    attention[...] = jnp.concatenate(joined, axis=0).T.astype(bf16)
    rows = [piece for log in logs for piece in log_pieces(log)]
    rows.append(jnp.zeros((LANES - len(rows), frames), f32))
    stats[...] = jnp.concatenate(rows, axis=0).T.astype(bf16)
    for send in sends:
        send.wait_send()


def log_pieces(log):
    high, middle, low = pieces(-log)
    return [high.astype(f32), middle.astype(f32), low.astype(f32)]


def forward_attention(modulated, w_q, w_k, w_v, key_aug, query_aug):
    frames, width = modulated.shape
    count = key_aug.shape[0]
    head_size = width // HEADS
    vmem = pl.BlockSpec(memory_space=pltpu.VMEM)
    shapes = (
        jax.ShapeDtypeStruct((frames, width), bf16),
        jax.ShapeDtypeStruct((frames, LANES), bf16),
        jax.ShapeDtypeStruct((count, frames, width), bf16),
        jax.ShapeDtypeStruct((frames, width), bf16),
        jax.ShapeDtypeStruct((count, 2, HEADS, frames, LANES), bf16),
        jax.ShapeDtypeStruct((HEADS, 2 * frames, LANES), bf16),
    )
    return pl.pallas_call(
        functools.partial(forward_kernel, frames, count),
        name="attention_forward",
        out_shape=shapes,
        in_specs=[vmem] * 6,
        out_specs=(vmem,) * 6,
        scratch_shapes=[
            pltpu.VMEM((HEADS, LANES, 2 * frames), f32),
            pltpu.VMEM((HEADS, 8, 2 * frames), f32),
            pltpu.VMEM((width, frames), bf16),
            pltpu.VMEM((width, frames), bf16),
            pltpu.VMEM((16, frames), f32),
            pltpu.VMEM((16, frames), f32),
            pltpu.SemaphoreType.DMA((2 + count,)),
            pltpu.SemaphoreType.DMA((3 + count,)),
        ],
        compiler_params=pltpu.CompilerParams(
            collective_id=1, has_side_effects=True, vmem_limit_bytes=62 * 2**20
        ),
    )(modulated, w_q, w_k, w_v, key_aug, query_aug)


def backward_kernel(
    frames,
    count,
    grad_att,
    attention,
    stats,
    mod_all,
    mod_peer,
    pairs,
    queries_in,
    w_qkv,
    spread_q,
    spread_o,
    sum_heads,
    grad_mod,
    grad_w,
    pack_out,
    pack_in,
    queries,
    grads,
    query_grad,
    key_grad,
    value_grad,
    flat_kv,
    part_out,
    part_in,
    peer_out,
    peer_in,
    held,
    held_sem,
    send_sem,
    recv_sem,
):
    batch, frame, side, column, peer = place()
    width = grad_att.shape[1]
    head_size = width // HEADS

    def block_at(step):
        return jnp.where(step == count, column, nearest(count - step, column, count))

    def fetch(step):
        slot = lax.rem(step - 1, 2)
        return pltpu.make_async_copy(
            pairs.at[block_at(step)], held.at[slot], held_sem.at[slot]
        )

    fetch(1).start()
    fetch(2).start()
    greet(batch, side, column, count, peer)

    def to_peer(source, target, slot):
        return pltpu.make_async_remote_copy(
            src_ref=source,
            dst_ref=target,
            send_sem=send_sem.at[slot],
            recv_sem=recv_sem.at[slot],
            device_id=(batch, peer),
            device_id_type=MESH,
        )

    def to_owner(step, owner, slot):
        return pltpu.make_async_remote_copy(
            src_ref=part_out.at[step],
            dst_ref=part_in.at[slot],
            send_sem=send_sem.at[2 + step],
            recv_sem=recv_sem.at[2 + slot],
            device_id=(batch, 2 * owner + side),
            device_id_type=MESH,
        )

    grad_now = grad_att[...]
    product = grad_now.astype(f32) * attention[...].astype(f32)
    high, middle, low = pieces(product)
    delta = (
        dg(high, sum_heads[...], NN) + dg(middle, sum_heads[...], NN) + dg(low, sum_heads[...], NN)
    )
    high, middle, low = pieces(-delta)
    pack_out[:, :width] = grad_now
    pack_out[:, width : width + LANES] = stats[...]
    pack_out[:, width + LANES : width + 2 * LANES] = high
    pack_out[:, width + 2 * LANES : width + 3 * LANES] = middle
    pack_out[:, width + 3 * LANES :] = low
    swap = to_peer(pack_out, pack_in, 0)
    swap.start()
    query_grad[...] = jnp.zeros_like(query_grad)

    def prepare(half, source):
        rows = pl.ds(half * frames, frames)
        wide = dg(source[:, :width], spread_o[:width, :], NN)
        wide += dg(source[:, width + LANES :], spread_o[width:, :], NN)
        extra = dg(source[:, width : width + LANES], spread_q[...], NN).astype(bf16)
        wide = wide.astype(bf16)
        for head in range(HEADS):
            lanes = slice(head * LANES, (head + 1) * LANES)
            grads[head, rows, :] = wide[:, lanes]
            queries[head, rows, :] = queries_in[head, rows, :] + extra[:, lanes]

    def differentiate(half, slot, first):
        rows = pl.ds(half * frames, frames)
        for head in range(HEADS):
            key, value = held[slot, 0, head], held[slot, 1, head]
            query, grad = queries[head, rows, :], grads[head, rows, :]
            probs = jnp.exp(dg(key, query, NT))
            dscore = (probs * dg(value, grad, NT)).astype(bf16)
            probs = probs.astype(bf16)
            more_k, more_v = dg(dscore, query, NN), dg(probs, grad, NN)
            if first:
                key_grad[slot, head] = more_k
                value_grad[slot, head] = more_v
            else:
                key_grad[slot, head] += more_k
                value_grad[slot, head] += more_v
            query_grad[head, :, rows] += dg(key, dscore, TN)

    def finish_keys(block, slot):
        for kind, source in enumerate((key_grad, value_grad)):
            for pair in range(HEADS // 2):
                start = kind * width + pair * LANES
                flat_kv[:, start : start + LANES] = jnp.concatenate(
                    [
                        source[slot, 2 * pair][:, :head_size],
                        source[slot, 2 * pair + 1][:, :head_size],
                    ],
                    axis=1,
                ).astype(bf16)
        flat = flat_kv[...]
        return dg(flat, w_qkv[:, width:], NT), dg(mod_all[block], flat, TN)

    def finish_queries(half, source):
        rows = pl.ds(half * frames, frames)
        flat = jnp.concatenate(
            [query_grad[head, :head_size, rows] for head in range(HEADS)], axis=0
        )
        flat = (flat * 0.125).T.astype(bf16)
        return dg(flat, w_qkv[:, :width], NT), dg(source, flat, TN)

    def send_block(step, slot, first):
        block = block_at(step)
        part, weight = finish_keys(block, slot)
        part_out[step] = part.astype(bf16)
        to_owner(step, block, column).start()
        if first:
            grad_w[:, width:] = weight
        else:
            grad_w[:, width:] += weight

        @pl.when(step + 2 <= count)
        def _():
            fetch(step + 2).start()

    prepare(0, pack_out[...])
    fetch(1).wait()
    differentiate(0, 0, True)
    fetch(2).wait()
    differentiate(0, 1, True)
    swap.wait()
    prepare(1, pack_in[...])
    differentiate(1, 0, False)
    send_block(1, 0, True)
    differentiate(1, 1, False)
    send_block(2, 1, False)

    def per_block(step, unused):
        slot = lax.rem(step - 1, 2)
        fetch(step).wait()
        differentiate(0, slot, True)
        differentiate(1, slot, False)
        send_block(step, slot, False)
        return unused

    lax.fori_loop(3, count, per_block, 0)
    slot = (count - 1) % 2
    fetch(count).wait()
    differentiate(1, slot, True)
    part, weight = finish_queries(1, mod_peer[...])
    peer_out[...] = part.astype(bf16)
    back = to_peer(peer_out, peer_in, 1)
    back.start()
    grad_w[:, :width] = weight
    differentiate(0, slot, False)
    part, weight = finish_keys(column, slot)
    grad_w[:, width:] += weight
    mine, weight = finish_queries(0, mod_all[column])
    grad_w[:, :width] += weight
    grad_mod[...] = part + mine

    def receive(step, unused):
        other = nearest(step, column, count)
        to_owner(step, other, other).wait_recv()
        grad_mod[...] += part_in[other].astype(f32)
        return unused

    lax.fori_loop(1, count, receive, 0)
    back.wait()
    grad_mod[...] += peer_in[...].astype(f32)

    def sent(step, unused):
        to_owner(step, column, column).wait_send()
        return unused

    lax.fori_loop(1, count, sent, 0)


def backward_attention(
    grad_att, attention, stats, mod_all, mod_peer, pairs, queries, w_qkv, spreads
):
    frames, width = grad_att.shape
    count = pairs.shape[0]
    vmem = pl.BlockSpec(memory_space=pltpu.VMEM)
    return pl.pallas_call(
        functools.partial(backward_kernel, frames, count),
        name="attention_backward",
        out_shape=(
            jax.ShapeDtypeStruct((frames, width), f32),
            jax.ShapeDtypeStruct((width, 3 * width), f32),
        ),
        in_specs=[vmem] * 5 + [pl.BlockSpec(memory_space=pl.ANY)] + [vmem] * 5,
        out_specs=(vmem,) * 2,
        scratch_shapes=[
            pltpu.VMEM((frames, width + 4 * LANES), bf16),
            pltpu.VMEM((frames, width + 4 * LANES), bf16),
            pltpu.VMEM((HEADS, 2 * frames, LANES), bf16),
            pltpu.VMEM((HEADS, 2 * frames, LANES), bf16),
            pltpu.VMEM((HEADS, LANES, 2 * frames), f32),
            pltpu.VMEM((2, HEADS, frames, LANES), f32),
            pltpu.VMEM((2, HEADS, frames, LANES), f32),
            pltpu.VMEM((frames, 2 * width), bf16),
            pltpu.VMEM((count, frames, width), bf16),
            pltpu.VMEM((count, frames, width), bf16),
            pltpu.VMEM((frames, width), bf16),
            pltpu.VMEM((frames, width), bf16),
            pltpu.VMEM((2, 2, HEADS, frames, LANES), bf16),
            pltpu.SemaphoreType.DMA((2,)),
            pltpu.SemaphoreType.DMA((2 + count,)),
            pltpu.SemaphoreType.DMA((2 + count,)),
        ],
        compiler_params=pltpu.CompilerParams(
            collective_id=2, has_side_effects=True, vmem_limit_bytes=62 * 2**20
        ),
    )(grad_att, attention, stats, mod_all, mod_peer, pairs, queries, w_qkv, *spreads)


def ids_at(positions, clip_ends):
    return jnp.sum((positions[..., None] >= clip_ends).astype(jnp.int32), axis=-1)


def split_heads(matrix, head_count):
    return matrix.reshape(matrix.shape[0], head_count, matrix.shape[1] // head_count).transpose(
        1, 0, 2
    )


def join_heads(stacked):
    return stacked.transpose(1, 0, 2).reshape(stacked.shape[1], stacked.shape[0] * stacked.shape[2])


def masked_scores(queries_h, keys_h, key_ids, query_ids, clip_count):
    head_size = queries_h.shape[2]
    scores = jnp.einsum(
        "hqd,hkd->hqk", queries_h, keys_h, preferred_element_type=jnp.float32
    ) * head_size ** (-0.5)
    allowed = (query_ids[:, None] == key_ids[None, :]) & (key_ids[None, :] < clip_count)
    return jnp.where(allowed[None], scores, MASKED)


def head_pad(weight):
    width = weight.shape[0]
    heads = weight.reshape(width, HEADS, -1)
    return jnp.pad(heads, ((0, 0), (0, 0), (0, LANES - heads.shape[2]))).reshape(
        width, HEADS * LANES
    )


def spread_matrices(width):
    head_size = width // HEADS
    lane = jnp.arange(HEADS * LANES, dtype=jnp.int32)[None, :]
    head, inner = lane // LANES, lane % LANES
    row = jnp.arange(LANES, dtype=jnp.int32)[:, None]
    spread_q = (row < 3 * HEADS) & (head == row // 3) & (inner == head_size + 4 + row % 3)
    row = jnp.arange(width, dtype=jnp.int32)[:, None]
    spread_o = [(head == row // head_size) & (inner == row % head_size)]
    row = jnp.arange(LANES, dtype=jnp.int32)[:, None]
    for piece in range(3):
        spread_o.append((row == head) & (inner == head_size + piece))
    column = jnp.arange(LANES, dtype=jnp.int32)[None, :]
    sum_heads = jnp.arange(width, dtype=jnp.int32)[:, None] // head_size == column
    return (
        spread_q.astype(bf16),
        jnp.concatenate(spread_o, axis=0).astype(bf16),
        sum_heads.astype(bf16),
    )


def per_device(
    latents,
    time_embed,
    text_states,
    text_len,
    clip_len,
    cotangent,
    w_ada,
    b_ada,
    w_qkv,
    w_ao,
    gain_cross,
    w_cq,
    w_ckv,
    w_co,
    w_up,
    w_down,
):
    frames = latents.shape[1]
    width = latents.shape[2]
    clip_count = time_embed.shape[1]
    text_slots = text_states.shape[2]
    head_size = width // HEADS
    score_scale = head_size ** (-0.5)
    frame = lax.axis_index("frame")
    count = lax.axis_size("frame") // 2
    side = frame % 2
    clip_ends = jnp.cumsum(clip_len[0])
    clips = jnp.arange(clip_count, dtype=jnp.int32)
    inner = jnp.arange(frames, dtype=jnp.int32)
    local_ids = ids_at(frame * frames + inner, clip_ends)
    peer_ids = ids_at((frame + 1 - 2 * side) * frames + inner, clip_ends)
    frame_valid = (local_ids < clip_count).astype(f32)[:, None]
    onehot = (local_ids[:, None] == clips[None, :]).astype(f32)

    lane = jnp.arange(LANES, dtype=jnp.int32)
    starts = (2 * jnp.arange(count, dtype=jnp.int32) + side) * frames
    key_ids = ids_at(starts[:, None] + inner[None, :], clip_ends)[..., None]
    masks = (lane >= head_size) & (lane < head_size + clip_count)
    key_aug = jnp.where(
        masks,
        jnp.where(key_ids == lane - head_size, 0.0, MASKED),
        jnp.where((lane >= head_size + 4) & (lane < head_size + 7), 1.0, 0.0),
    ).astype(bf16)
    query_ids = jnp.concatenate([local_ids, peer_ids])[:, None]
    query_aug = (masks & (query_ids == lane - head_size)).astype(bf16)

    inputs = latents[0].astype(f32)
    time_low = jax.nn.silu(time_embed[0].astype(f32)).astype(bf16)
    modulation = jnp.dot(time_low, w_ada, preferred_element_type=f32) + b_ada
    frame_mod = jnp.dot(onehot, modulation, precision=highest)
    shift_attn, scale_attn, gate_attn, shift_mlp, scale_mlp, gate_mlp = jnp.split(
        frame_mod, 6, axis=1
    )
    normed_attn, inverse_attn = layer_norm(inputs)
    modulated = (normed_attn * (1.0 + scale_attn) + shift_attn).astype(bf16)
    attention, stats, mod_all, mod_peer, pairs, queries = forward_attention(
        modulated,
        head_pad(w_qkv[:, :width]),
        head_pad(w_qkv[:, width : 2 * width]),
        head_pad(w_qkv[:, 2 * width :]),
        key_aug,
        query_aug,
    )

    branch_attn = jnp.dot(attention, w_ao, preferred_element_type=f32)
    after_attn = inputs + gate_attn * branch_attn * frame_valid
    normed_cross, inverse_cross = layer_norm(after_attn)
    cross_in = (normed_cross * gain_cross).astype(bf16)
    cross_queries = jnp.dot(cross_in, w_cq, preferred_element_type=f32).astype(bf16)
    text_rows = text_states[0].reshape(clip_count * text_slots, text_states.shape[3])
    text_kv = jnp.dot(text_rows, w_ckv, preferred_element_type=f32).astype(bf16)
    text_keys_h = split_heads(text_kv[:, :width], HEADS)
    text_values_h = split_heads(text_kv[:, width:], HEADS)
    slot_rows = jnp.arange(clip_count * text_slots, dtype=jnp.int32)
    text_clip = slot_rows // text_slots
    text_live = slot_rows % text_slots < jnp.repeat(text_len[0], text_slots)
    text_clip = jnp.where(text_live, text_clip, clip_count)
    cross_queries_h = split_heads(cross_queries, HEADS)
    cross_scores = masked_scores(cross_queries_h, text_keys_h, text_clip, local_ids, clip_count)
    cross_probs = jax.nn.softmax(cross_scores, axis=-1)
    cross_low = cross_probs.astype(bf16)
    cross = join_heads(
        jnp.einsum("hqk,hkd->hqd", cross_low, text_values_h, preferred_element_type=f32)
    ).astype(bf16)
    branch_cross = jnp.dot(cross, w_co, preferred_element_type=f32)
    after_cross = after_attn + branch_cross * frame_valid
    normed_mlp, inverse_mlp = layer_norm(after_cross)
    mlp_in = (normed_mlp * (1.0 + scale_mlp) + shift_mlp).astype(bf16)
    hidden = jnp.dot(mlp_in, w_up, preferred_element_type=f32)
    activated, gelu_pull = jax.vjp(lambda value: jax.nn.gelu(value, approximate=True), hidden)
    activated = activated.astype(bf16)
    branch_mlp = jnp.dot(activated, w_down, preferred_element_type=f32)
    mixed = after_cross + gate_mlp * branch_mlp * frame_valid
    grad_out = cotangent[0].astype(f32)
    grad_mlp = (grad_out * gate_mlp * frame_valid).astype(bf16)
    grad_gate_mlp = grad_out * branch_mlp * frame_valid
    grad_w_down = jnp.dot(activated.T, grad_mlp, preferred_element_type=f32)
    grad_act = jnp.dot(grad_mlp, w_down.T, preferred_element_type=f32)
    grad_hidden = gelu_pull(grad_act)[0].astype(bf16)
    grad_w_up = jnp.dot(mlp_in.T, grad_hidden, preferred_element_type=f32)
    grad_mlp_in = jnp.dot(grad_hidden, w_up.T, preferred_element_type=f32)
    grad_cross_out = grad_out + norm_back(grad_mlp_in * (1.0 + scale_mlp), normed_mlp, inverse_mlp)
    grad_branch_cross = (grad_cross_out * frame_valid).astype(bf16)
    grad_w_co = jnp.dot(cross.T, grad_branch_cross, preferred_element_type=f32)
    grad_cross_h = split_heads(
        jnp.dot(grad_branch_cross, w_co.T, preferred_element_type=f32).astype(bf16), HEADS
    )
    cross_dprob = jnp.einsum(
        "hqd,hkd->hqk", grad_cross_h, text_values_h, preferred_element_type=f32
    )
    cross_dscore = (
        cross_probs * (cross_dprob - jnp.sum(cross_probs * cross_dprob, axis=-1, keepdims=True))
    ).astype(bf16)
    grad_cross_queries = (
        join_heads(
            jnp.einsum("hqk,hkd->hqd", cross_dscore, text_keys_h, preferred_element_type=f32)
        )
        * score_scale
    ).astype(bf16)
    grad_text_keys = (
        join_heads(
            jnp.einsum("hqk,hqd->hkd", cross_dscore, cross_queries_h, preferred_element_type=f32)
        )
        * score_scale
    )
    grad_text_values = join_heads(
        jnp.einsum("hqk,hqd->hkd", cross_low, grad_cross_h, preferred_element_type=f32)
    )
    grad_text = jnp.concatenate([grad_text_keys, grad_text_values], axis=1).astype(bf16)
    grad_w_ckv = jnp.dot(text_rows.T, grad_text, preferred_element_type=f32)
    grad_w_cq = jnp.dot(cross_in.T, grad_cross_queries, preferred_element_type=f32)
    grad_cross_in = jnp.dot(grad_cross_queries, w_cq.T, preferred_element_type=f32)
    grad_gain_cross = jnp.sum(grad_cross_in * normed_cross, axis=0)
    grad_attn_out = grad_cross_out + norm_back(
        grad_cross_in * gain_cross, normed_cross, inverse_cross
    )
    grad_branch_attn = (grad_attn_out * gate_attn * frame_valid).astype(bf16)
    grad_gate_attn = grad_attn_out * branch_attn * frame_valid
    grad_w_ao = jnp.dot(attention.T, grad_branch_attn, preferred_element_type=f32)
    grad_attention = jnp.dot(grad_branch_attn, w_ao.T, preferred_element_type=f32).astype(bf16)

    both = ("batch", "frame")
    middle = (grad_w_ao, grad_w_cq, grad_w_ckv, grad_w_co, grad_w_up, grad_w_down)
    middle = lax.psum(tuple(grad.astype(bf16) for grad in middle), both)

    grad_mod_in, grad_w_qkv = backward_attention(
        grad_attention,
        attention,
        stats,
        mod_all,
        mod_peer,
        pairs,
        queries,
        w_qkv,
        spread_matrices(width),
    )
    middle, grad_w_qkv = lax.optimization_barrier((middle, grad_w_qkv))
    grad_inputs = grad_attn_out + norm_back(
        grad_mod_in * (1.0 + scale_attn), normed_attn, inverse_attn
    )
    grad_frame_mod = jnp.concatenate(
        [
            grad_mod_in,
            grad_mod_in * normed_attn,
            grad_gate_attn,
            grad_mlp_in,
            grad_mlp_in * normed_mlp,
            grad_gate_mlp,
        ],
        axis=1,
    )
    grad_modulation = jnp.dot(onehot.T, grad_frame_mod, precision=highest)
    time_all = lax.all_gather(time_low, "batch", axis=0, tiled=True)
    own_rows = (jnp.arange(lax.axis_size("batch")) == lax.axis_index("batch")).astype(f32)
    spread_rows = (own_rows[:, None, None] * grad_modulation[None]).reshape(-1, 6 * width)
    grad_w_qkv = lax.psum(grad_w_qkv.astype(bf16), both)
    spread_rows, grad_gain_cross = lax.psum((spread_rows, grad_gain_cross), both)
    grad_w_ada = jnp.dot(time_all.astype(f32).T, spread_rows, precision=highest)
    grad_b_ada = jnp.sum(spread_rows, axis=0)
    grad_w_ao, grad_w_cq, grad_w_ckv, grad_w_co, grad_w_up, grad_w_down = (
        grad.astype(f32) for grad in middle
    )
    return (
        mixed.astype(bf16)[None],
        grad_inputs.astype(bf16)[None],
        grad_w_ada,
        grad_b_ada,
        grad_w_qkv.astype(f32),
        grad_w_ao,
        grad_gain_cross,
        grad_w_cq,
        grad_w_ckv,
        grad_w_co,
        grad_w_up,
        grad_w_down,
    )


def solution(mesh):
    placed = (
        P("batch", "frame", None),
        P("batch", None, None),
        P("batch", None, None, None),
        P("batch", None),
        P("batch", None),
        P("batch", "frame", None),
    ) + (P(),) * 10
    return jax.shard_map(
        per_device,
        mesh=mesh,
        in_specs=placed,
        out_specs=(P("batch", "frame", None), P("batch", "frame", None)) + (P(),) * 10,
        check_vma=False,
    )
```

time: 774 us -> 583 us (0.75)
  matrix products: 267 us -> 50.5 us
  Pallas kernels: 0 us -> 134 us
  local copies, waits for them, and re-layouts: 73.2 us -> 9.6 us
  waiting for transfers between devices: 311 us -> 274 us
  other arithmetic: 59.7 us -> 45.3 us
    dot_general x50 -> x19, matrix products: 244 us -> 28.4 us  [the longest x1 4.36 us: per_device(): grad_w_ada = jnp.dot(time_all.astype(f32).T, spread_rows, precision=highest)]
    pallas_call x0 -> x2, Pallas kernels: none -> 134 us  [the longest x1 69.5 us: backward_attention(): pl.pallas_call(functools.partial(backward_kernel, frames, count), name='a...]
    all_gather x1 -> x0, waiting for transfers between devices: 96 us -> none  [per_device(): segment = lax.all_gather(kv_local, 'frame', axis=0, tiled=True)]
    psum x1 -> x3, waiting for transfers between devices: 203 us -> 274 us  [the longest x1 122 us: per_device(): grad_w_qkv = lax.psum(grad_w_qkv.astype(bf16), both)]
    reduce_sum x7 -> x4, other arithmetic: 30.6 us -> 5.04 us  [the longest x1 2.72 us: norm_back(): mean_grad = jnp.mean(grad, axis=-1, keepdims=True)]
    unnamed x178 -> x100, local copies, waits for them, and re-layouts: 28.3 us -> 3.93 us
    squeeze x12 -> x0, local copies, waits for them, and re-layouts: 18.5 us -> none  [fold_keys(): return lax.scan(per_block, carried, (kv_blocks, id_blocks))[0]]
    convert_element_type x6 -> x16, other arithmetic: 4.43 us -> 17.7 us  [the longest x5 7.22 us: per_device(): grad.astype(f32)]
  transfers between devices with their start and end apart: 3 -> 3, of which waited for: 3 -> 3; matrix products, arithmetic and copies ran while one was open for 14% -> 6% of each run, Pallas kernels for 0% -> 12%
where the time goes in v1:
time: 583 us; the launch traced here: 574 us
  waiting for transfers between devices  274 us (47%)
  Pallas kernels  134 us (23%)
  matrix products  50.5 us (9%)
  other arithmetic  45.3 us (8%)
  blocking collectives  44.9 us (8%)
  between operations  14.7 us (3%)
  local copies, waits for them, and re-layouts  9.6 us (2%)
    psum x1, waiting for transfers between devices, per_device(): grad_w_qkv = lax.psum(grad_w_qkv.astype(bf16), both)  122 us
    psum x1, waiting for transfers between devices, per_device(): lax.psum((spread_rows, grad_gain_cross), both)  80.3 us
    psum x1, waiting for transfers between devices, per_device(): middle = lax.psum(tuple((grad.astype(bf16) for grad in middle)), both)  71.8 us
    pallas_call x1, Pallas kernels, backward_attention(): pl.pallas_call(functools.partial(backward_kernel, frames, count), name='a...  69.5 us
    pallas_call x1, Pallas kernels, forward_attention(): pl.pallas_call(functools.partial(forward_kernel, frames, count), name='at...  64.8 us
    psum x1, blocking collectives, per_device(): lax.psum((spread_rows, grad_gain_cross), both)  39.6 us
  transfers between devices with their start and end apart: 3, of which 3 were waited for; matrix products, arithmetic and copies ran while one was open for 6% of the time, Pallas kernels for 12%

profile of v1, /device:TPU:0, one launch (start us, length us, event | category | flops | bytes accessed | tf_op | source)
XLA Modules:
  0.0 573.7 jit_solution(447941722675903614)
XLA Ops:
  8.8 0.8 reduce-window.8
  9.6 1.1 convert_reduce_fusion
  10.8 1.2 fusion.42
  12.1 1.3 broadcast_compare_fusion.3
  14.2 0.7 convert_reduce_fusion.1
  14.8 1.9 convolution_convert_fusion.3
  16.8 0.9 copy.98
  17.7 0.9 copy.99
  19.1 1.1 copy.96.w_vp
  20.4 1.1 copy.95.w_kp
  21.8 1.1 copy.94.w_qp
  23.3 2.1 fusion.61
  25.4 0.9 and_convert_fusion.query_aug
  26.3 1.5 select_convert_fusion.key_aug
  27.8 1.0 fusion.35.mod_own
  28.8 64.8 %attention_forward.1 = (bf16[512,384]{1,0:T(8,128)(2,1)}, bf16[512,128]{1,0:T(8,128)(2,1)}, bf16[4,512,384]{2,1,0:T(8,128)(2,1)}, bf16[512,384]{1,0:T(8,128)(2,1...) custom-call(bf16[512,384]{1,0:T(8,128)(2,1)} %fusion.35.mod_own, bf16[384,768]{1,0:T(8,128)(2,1)} %copy.94.w_qp, ...), custom_call_target="tpu_custom_call" | custom-call | tf_op jit(solution)/shard_map/attention_forward/pallas_call | solution.py:252
  93.7 3.0 fusion.98
  97.8 5.1 fusion.103
  102.9 3.6 fusion.20
  107.9 1.0 fusion.105
  109.2 1.1 fusion.97
  110.3 2.8 convolution_convert_fusion
  113.1 2.5 fusion.8
  115.6 1.8 convolution_convert_fusion.1
  117.5 1.1 fusion.95
  118.6 1.3 convert_add_fusion
  119.9 1.2 convolution_convert_fusion.7
  121.6 1.8 fusion.23
  123.4 3.7 multiply_reduce_fusion
  127.1 4.5 multiply_convert_fusion
  131.7 1.1 fusion.18
  133.4 1.3 convolution_convert_fusion.8
  134.7 0.7 multiply_reduce_fusion.1
  135.5 1.3 multiply_convert_fusion.2
  136.8 1.1 convolution_convert_fusion.9
  137.9 1.4 fusion.16
  139.7 1.2 convolution_convert_fusion.4.grad_att
  140.9 0.8 fusion.62.sum_heads
  141.9 1.0 fusion.59
  142.9 1.2 add_convert_fusion.spread_o
  144.2 69.5 %attention_backward.1 = (f32[512,384]{1,0:T(8,128)}, f32[384,1152]{1,0:T(8,128)}) custom-call(bf16[512,384]{1,0:T(8,128)(2,1)} %convolution_convert_fusion.4.grad_att, bf16[512,384]{1,0:T(8,128)(2,1)} %get-tuple-element.27.attention, bf16[512,128]{1,0:T(8,128)(2,1)} %get-tuple-element.28.stats, bf16[4,512,384]{2,1,0:T(8,128)(2,1)} %get-tuple-element.29.mod_all, ...), custom_call_target="tpu_custom_call" | custom-call | tf_op jit(solution)/shard_map/attention_backward/pallas_call | solution.py:483
  213.7 2.7 fusion.96
  216.4 2.6 fusion.41
  219.2 2.3 multiply_dynamic-update-slice_fusion.1
  221.5 1.0 constant_dynamic-update-slice_fusion
  222.6 1.1 multiply_dynamic-update-slice_fusion
  223.7 1.1 fusion.46
  224.8 4.1 fusion.60
  229.0 0.7 broadcast_multiply_fusion
  229.8 71.8 %all-reduce.12.cloned.1.call-done = (bf16[384,384]{1,0:T(8,128)(2,1)}, bf16[384,384]{1,0:T(8,128)(2,1)}, bf16[512,768]{0,1:T(8,128)(2,1)}, bf16[384,384]{1,0:T(8...) async-done(((bf16[384,384]{1,0:T(8,128)(2,1)}, bf16[384,384]{1,0:T(8,128)(2,1)}, bf16[512,768]{0,1:T(8,128)(2,1)}, bf16[384,384]{1,0:T(8,128)(2,1)}, ...) | async-done | bytes 4030480 | tf_op jit(solution)/shard_map/psum | solution.py:711
  301.6 1.0 convert_element_type.223
  302.7 5.3 all-gather
  308.0 39.6 %psum.71 = f32[384]{0:T(512)} all-reduce(f32[384]{0:T(512)S(1)} %get-tuple-element.94), channel_id=1, replica_groups=mesh['batch'=4,'frame'=8] {'batch','frame'}, use_global_device_ids=true, to_apply=%region_29.30 | all-reduce | flops 384 | bytes 3072 | tf_op jit(solution)/shard_map/psum | solution.py:744
  347.6 80.3 %all-reduce.8.cloned.1.call-done = f32[16,2304]{1,0:T(8,128)} async-done(((f32[16,2304]{1,0:T(8,128)}), f32[16,2304]{1,0:T(8,128)}) %all-reduce.8.cloned.1.call-update) | async-done | bytes 147472 | tf_op jit(solution)/shard_map/psum | solution.py:744
  427.9 1.5 reduce_sum.188
  429.4 4.4 fusion.106
  433.8 0.9 convert_element_type.225
  434.6 0.9 convert_element_type.226
  435.5 0.9 convert_element_type.228
  436.3 1.4 copy.113
  437.8 3.1 convert_element_type.229
  440.9 1.6 convert_element_type.230
  442.4 122.0 %all-reduce.10.cloned.1.call-done = bf16[384,1152]{1,0:T(8,128)(2,1)} async-done(((bf16[384,1152]{1,0:T(8,128)(2,1)}), bf16[384,1152]{1,0:T(8,128)(2,1)}) %all-reduce.10.cloned.1.call-update) | async-done | bytes 884752 | tf_op jit(solution)/shard_map/psum | solution.py:743
  564.5 2.5 convert_element_type.224
  (154 shorter events, 8.6 us)
Async XLA Ops:
  7.2 15.7 %copy-start = (bf16[384,2304]{1,0:T(8,128)(2,1)S(1)}, bf16[384,2304]{1,0:T(8,128)(2,1)}, u32[]{:S(2)}) copy-start(bf16[384,2304]{1,0:T(8,128)(2,1)} %param.22) | copy-start | bytes 5308420
  7.2 294.4 %all-reduce.12.cloned.1.call-start = ((), (), s32[]{:S(2)}) async-start(), calls=%async_computation.2 | async-start | bytes 8060928 | tf_op jit(solution)/shard_map/psum | solution.py:711
  7.2 11.4 %copy-start.8 = (bf16[384,1152]{1,0:T(8,128)(2,1)S(1)}, bf16[384,1152]{1,0:T(8,128)(2,1)}, u32[]{:S(2)}) copy-start(bf16[384,1152]{1,0:T(8,128)(2,1)} %w_qkv.1) | copy-start | bytes 2654212
  19.1 3.8 copy-start.33
  19.1 3.8 copy-start.34
  22.9 2.5 copy-start.32
  22.9 2.5 copy-start.36
  22.9 2.5 copy-start.37
  22.9 3.4 copy-start.30
  22.9 3.4 copy-start.39
  23.3 4.5 copy-start.3
  25.4 2.4 copy-start.2
  25.4 68.3 %copy-start.9 = (bf16[1,512,384]{2,1,0:T(8,128)(2,1)S(1)}, bf16[1,512,384]{2,1,0:T(8,128)(2,1)}, u32[]{:S(2)}) copy-start(bf16[1,512,384]{2,1,0:T(8,128)(2,1)} %param.21) | copy-start | bytes 1179652
  93.6 3.3 copy-start.35
  93.6 3.3 copy-start.38
  93.7 3.5 copy-start.28
  93.7 3.5 copy-start.31
  93.7 4.1 copy-start.17
  97.8 5.1 copy-start.23
  97.8 9.5 %slice-start = ((s8[4718592]{0:T(1024)(128)(4,1)}), s8[524288]{0:T(1024)(128)(4,1)S(1)}, s32[]{:S(2)}) async-start(s8[4718592]{0:T(1024)(128)(4,1)} %bitcast.141), calls=%async_computation.3 | async-start | bytes 1048576
  102.9 3.6 copy-start.20
  102.9 4.4 slice-start.1
  106.5 1.4 copy-start.18
  107.9 1.3 copy-start.40
  110.3 8.3 %copy-start.12 = (f32[512,384]{1,0:T(8,128)}, f32[512,384]{1,0:T(8,128)S(1)}, u32[]{:S(2)}) copy-start(f32[512,384]{1,0:T(8,128)S(1)} %fusion.97) | copy-start | bytes 2359300
  117.5 1.2 copy-start.10
  117.5 4.1 slice-start.2
  118.6 2.5 copy-start.5
  118.6 2.9 slice-start.3
  121.6 1.9 copy-start.24
  132.7 2.0 copy-start.29
  134.7 2.1 copy-start.16
  135.5 2.5 copy-start.41
  135.5 2.5 copy-start.42
  137.9 1.8 copy-start.21
  139.4 288.5 %all-reduce.8.cloned.1.call-start = ((), (), s32[]{:S(2)}) async-start(), calls=%async_computation | async-start | bytes 294912 | tf_op jit(solution)/shard_map/psum | solution.py:744
  144.2 69.5 %copy-start.4 = (bf16[1,512,384]{2,1,0:T(8,128)(2,1)S(1)}, bf16[1,512,384]{2,1,0:T(8,128)(2,1)}, u32[]{:S(2)}) copy-start(bf16[1,512,384]{2,1,0:T(8,128)(2,1)} %param.16) | copy-start | bytes 1179652
  213.6 2.8 copy-start.7
  213.7 2.8 copy-start.14
  216.4 5.1 copy-start.6
  219.2 4.5 copy-start.11
  219.2 4.5 copy-start.13
  224.8 76.8 %copy-start.15 = (f32[384,1152]{1,0:T(8,128)S(1)}, f32[384,1152]{1,0:T(8,128)}, u32[]{:S(2)}) copy-start(f32[384,1152]{1,0:T(8,128)} %get-tuple-element.35) | copy-start | bytes 5308420
  229.8 334.7 %all-reduce.10.cloned.1.call-start = ((), (), s32[]{:S(2)}) async-start(), calls=%async_computation.1 | async-start | bytes 1769472 | tf_op jit(solution)/shard_map/psum | solution.py:743
  301.6 132.2 %copy-start.27 = (bf16[384,384]{1,0:T(8,128)(2,1)S(1)}, bf16[384,384]{1,0:T(8,128)(2,1)}, u32[]{:S(2)}) copy-start(bf16[384,384]{1,0:T(8,128)(2,1)} %get-tuple-element.36) | copy-start | bytes 884740
  302.6 132.0 %copy-start.26 = (bf16[384,384]{1,0:T(8,128)(2,1)S(1)}, bf16[384,384]{1,0:T(8,128)(2,1)}, u32[]{:S(2)}) copy-start(bf16[384,384]{1,0:T(8,128)(2,1)} %get-tuple-element.37) | copy-start | bytes 884740
  302.6 132.9 %copy-start.25 = (bf16[384,384]{1,0:T(8,128)(2,1)S(1)}, bf16[384,384]{1,0:T(8,128)(2,1)}, u32[]{:S(2)}) copy-start(bf16[384,384]{1,0:T(8,128)(2,1)} %get-tuple-element.39) | copy-start | bytes 884740
  429.4 6.9 %copy-start.22 = (bf16[512,768]{0,1:T(8,128)(2,1)S(1)}, bf16[512,768]{0,1:T(8,128)(2,1)}, u32[]{:S(2)}) copy-start(bf16[512,768]{0,1:T(8,128)(2,1)} %get-tuple-element.38) | copy-start | bytes 2359300
  436.3 4.5 copy-start.19
  437.8 129.2 %copy-start.1 = (bf16[384,2304]{1,0:T(8,128)(2,1)S(1)}, bf16[384,2304]{1,0:T(8,128)(2,1)}, u32[]{:S(2)}) copy-start(bf16[384,2304]{1,0:T(8,128)(2,1)} %param.22) | copy-start | bytes 5308420
Sparse Core Ops, SparseCore 0:
  139.5 162.0 all-reduce.11
  307.7 120.1 all-reduce.7
  433.7 130.7 all-reduce.9
